TPU v7x, 512 devices: a whole 4x8x8 slice. The times are simulated.
512 devices in a mesh: ctx: 128 (over z, x, y_lo), tp: 4 (over y_hi, core).
Axes of the slice: x: 4, y: 8 (y_hi: 2, y_lo: 4; y = y_hi * 4 + y_lo), z: 8, core: 2. Of those that a mesh axis runs over, the one named last changes fastest.
Arguments:
- self_queries: bfloat16 [16384, 8192], P('ctx', 'tp'), may hold values from -1000 to 1000
- cross_queries: bfloat16 [16384, 8192], P('ctx', 'tp'), may hold values from -1000 to 1000
- text_pairs: bfloat16 [2, 16384, 1024], P(None, 'ctx', 'tp'), may hold values from -4 to 4
- image_pairs: bfloat16 [2, 256, 128, 1024], P(None, 'ctx', 'tp'), may hold values from -4 to 4
- doc_lengths: int32 [64], replicated, may hold values from 1 to 385, 16384 in all
- image_places: int32 [256], replicated, may hold values from -1 to 16383, as said below
Outputs:
- self_out: bfloat16 [16384, 8192], P('ctx', 'tp')
- cross_out: bfloat16 [16384, 8192], P('ctx', 'tp')
Inputs may be any that keep to these rules, and one draw needn't show every extreme that they name: `doc_lengths`: they sum to 16384; the longest document has exactly 385 tokens. `image_places`: entry s is -1 for an empty slot, else the position of its image in the token order, which lies in context block s // 2; the positions are distinct.
All inputs are finite; a program needn't handle non-finite values.
Results may differ from a plain program's by a relative error of at most 0.0054.
Values may be sent and summed in bfloat16 or wider, within the bound.
A program may use at most 64 MiB of HBM per device.

v0:
```python
import jax
import jax.numpy as jnp
from jax import lax
from jax.sharding import PartitionSpec as P

HEAD_DIM = 128
SPAN = 4


masked_score = -1e30


def shifted(value, axis, steps):
    count = lax.axis_size(axis)
    initial, last = (max(0, -steps), min(count, count - steps))
    return lax.ppermute(value, axis, [(source, source + steps) for source in range(initial, last)])


def absorb(carried, queries, key_block, value_block, visible):
    running_max, running_sum, weighted = carried
    scores = jnp.einsum("tgrd,kgd->tgrk", queries, key_block, preferred_element_type=jnp.float32)
    scores = scores * HEAD_DIM ** (-0.5)
    shown_mask = visible[:, None, None, :]
    scores = jnp.where(shown_mask, scores, masked_score)
    new_max = jnp.maximum(running_max, jnp.max(scores, axis=-1))
    weights = jnp.where(shown_mask, jnp.exp(scores - new_max[..., None]), 0.0)
    factor = jnp.exp(running_max - new_max)
    running_sum = running_sum * factor + jnp.sum(weights, axis=-1)
    product = jnp.einsum(
        "tgrk,kgd->tgrd",
        weights.astype(jnp.bfloat16),
        value_block,
        preferred_element_type=jnp.float32,
    )
    weighted = weighted * factor[..., None] + product
    return (new_max, running_sum, weighted)


def finish(carried):
    running_max, running_sum, weighted = carried
    positive = running_sum > 0.0
    safe_sum = jnp.where(positive, running_sum, 1.0)
    result = jnp.where(positive[..., None], weighted / safe_sum[..., None], 0.0)
    return result.reshape(result.shape[0], -1).astype(jnp.bfloat16)


def per_device(self_queries, cross_queries, text_pairs, image_pairs, doc_lengths, image_places):
    row_count = self_queries.shape[0]
    group_count = text_pairs.shape[2] // HEAD_DIM
    head_ratio = self_queries.shape[1] // HEAD_DIM // group_count
    block_index = lax.axis_index("ctx")
    offsets = jnp.arange(row_count, dtype=jnp.int32)
    places = block_index * row_count + offsets
    doc_ends = jnp.cumsum(doc_lengths)
    doc_starts = doc_ends - doc_lengths
    inside = (doc_starts[None, :] <= places[:, None]) & (places[:, None] < doc_ends[None, :])
    doc_begin = jnp.sum(jnp.where(inside, doc_starts[None, :], 0), axis=1)
    self_query = self_queries.reshape(row_count, group_count, head_ratio, HEAD_DIM)
    cross_query = cross_queries.reshape(row_count, group_count, head_ratio, HEAD_DIM)
    images = lax.all_to_all(image_pairs, "tp", split_axis=3, concat_axis=2, tiled=True)
    slot_count = images.shape[1]
    image_rows = images.shape[2]

    def fresh_state():
        return (
            jnp.full((row_count, group_count, head_ratio), masked_score, jnp.float32),
            jnp.zeros((row_count, group_count, head_ratio), jnp.float32),
            jnp.zeros((row_count, group_count, head_ratio, HEAD_DIM), jnp.float32),
        )

    def take_block(states, text_block, image_block, source):
        key_places = source * row_count + offsets
        text_seen = (key_places[None, :] >= doc_begin[:, None]) & (
            key_places[None, :] <= places[:, None]
        )
        slot_start = jnp.maximum(source, 0) * slot_count
        slot_places = lax.dynamic_slice_in_dim(image_places, slot_start, slot_count)
        slot_places = jnp.where(source >= 0, slot_places, -1)
        token_places = jnp.repeat(slot_places, image_rows)
        image_seen = (token_places[None, :] >= doc_begin[:, None]) & (
            token_places[None, :] <= places[:, None]
        )
        text_keys = text_block[0].reshape(row_count, group_count, HEAD_DIM)
        text_values = text_block[1].reshape(row_count, group_count, HEAD_DIM)
        image_keys = image_block[0].reshape(slot_count * image_rows, group_count, HEAD_DIM)
        image_values = image_block[1].reshape(slot_count * image_rows, group_count, HEAD_DIM)
        self_state = absorb(states[0], self_query, text_keys, text_values, text_seen)
        cross_state = absorb(states[1], cross_query, image_keys, image_values, image_seen)
        return (self_state, cross_state)

    states = take_block((fresh_state(), fresh_state()), text_pairs, images, block_index)
    held_text = text_pairs
    held_image = images
    for hop_index in range(1, SPAN):
        held_text, held_image = shifted((held_text, held_image), "ctx", 1)
        states = take_block(states, held_text, held_image, block_index - hop_index)
    return (finish(states[0]), finish(states[1]))


def solution(mesh):
    placed = (
        P("ctx", "tp"),
        P("ctx", "tp"),
        P(None, "ctx", "tp"),
        P(None, "ctx", "tp", None),
        P(),
        P(),
    )
    return jax.shard_map(
        per_device,
        mesh=mesh,
        in_specs=placed,
        out_specs=(P("ctx", "tp"), P("ctx", "tp")),
        check_vma=False,
    )
```

profile of v0, /device:TPU:256, one launch (start us, length us, event | category | flops | bytes accessed | tf_op | source)
XLA Modules:
  0.0 115.5 jit_solution(8075038290688627455)
XLA Ops:
  0.7 2.3 %copy.158 = bf16[2,2,32,1024]{2,1,0,3:T(2,128)(2,1)S(1)} copy(bf16[2,2,32,1024]{3,2,1,0:T(8,128)(2,1)} %param.9) | data formatting | bytes 524288 | tf_op args[3]
  3.0 1.7 %reshape.656 = bf16[4,2,16384]{2,1,0:T(2,128)(2,1)} reshape(bf16[1024,2,2,32]{3,2,1,0:T(2,128)(2,1)S(1)} %bitcast.219) | data formatting | bytes 524288
  4.7 7.1 %all-to-all-start = ((bf16[4,2,16384]{2,1,0:T(2,128)(2,1)}), bf16[4,2,16384]{2,1,0:T(2,128)(2,1)S(1)}, u32[]{:S(2)}, u32[]{:S(2)}) async-start(bf16[4,2,16384]{2,1,0:T(2,128)(2,1)} %reshape.656), calls=%async_computation | async-start | bytes 524288 | tf_op jit(solution)/shard_map/all_to_all | solution.py:60
  11.9 2.6 %collective-permute-start = (bf16[2,128,256]{1,2,0:T(8,128)(2,1)S(1)}, bf16[2,128,256]{1,2,0:T(8,128)(2,1)S(1)}, u32[]{:S(2)}, u32[]{:S(2)}) collective-permute-start(bf16[2,128,256]{1,2,0:T(8,128)(2,1)S(1)} %copy.143), channel_id=1, source_target_pairs={{0,4},{4,8},{8,12},{12,16},{16,20},{20,24},{24,28},{28,32},{32,36}... | collective-permute-start | bytes 393224 | tf_op jit(solution)/shard_map/ppermute | solution.py:16
  15.8 0.4 fusion.140
  16.1 0.2 compare_and_fusion.2
  16.4 11.8 %collective-permute-done = bf16[2,128,256]{1,2,0:T(8,128)(2,1)S(1)} collective-permute-done((bf16[2,128,256]{1,2,0:T(8,128)(2,1)S(1)}, bf16[2,128,256]{1,2,0:T(8,128)(2,1)S(1)}, u32[]{:S(2)}, u32[]{:S(2)}) %collective-permute-start) | collective-permute-done | bytes 131104 | tf_op jit(solution)/shard_map/ppermute | solution.py:16
  28.2 1.9 %collective-permute-start.1 = (bf16[2,128,256]{1,2,0:T(8,128)(2,1)S(1)}, bf16[2,128,256]{1,2,0:T(8,128)(2,1)S(1)}, u32[]{:S(2)}, u32[]{:S(2)}) collective-permute-start(bf16[2,128,256]{1,2,0:T(8,128)(2,1)S(1)} %collective-permute-done), channel_id=1, source_target_pairs={{0,4},{4,8},{8,12},{12,16},{16,20},{20,24},{24,28},{28,32},{32,36}... | collective-permute-start | bytes 393224 | tf_op jit(solution)/shard_map/ppermute | solution.py:16
  30.1 0.4 fusion.139
  30.5 10.7 %collective-permute-done.1 = bf16[2,128,256]{1,2,0:T(8,128)(2,1)S(1)} collective-permute-done((bf16[2,128,256]{1,2,0:T(8,128)(2,1)S(1)}, bf16[2,128,256]{1,2,0:T(8,128)(2,1)S(1)}, u32[]{:S(2)}, u32[]{:S(2)}) %collective-permute-start.1) | collective-permute-done | bytes 131104 | tf_op jit(solution)/shard_map/ppermute | solution.py:16
  41.2 1.9 %collective-permute-start.2 = (bf16[2,128,256]{1,2,0:T(8,128)(2,1)S(1)}, bf16[2,128,256]{1,2,0:T(8,128)(2,1)S(1)}, u32[]{:S(2)}, u32[]{:S(2)}) collective-permute-start(bf16[2,128,256]{1,2,0:T(8,128)(2,1)S(1)} %collective-permute-done.1), channel_id=1, source_target_pairs={{0,4},{4,8},{8,12},{12,16},{16,20},{20,24},{24,28},{28,32},{32,36}... | collective-permute-start | bytes 393224 | tf_op jit(solution)/shard_map/ppermute | solution.py:16
  43.1 0.4 fusion.138
  43.5 10.6 %collective-permute-done.2 = bf16[2,128,256]{1,2,0:T(8,128)(2,1)S(1)} collective-permute-done((bf16[2,128,256]{1,2,0:T(8,128)(2,1)S(1)}, bf16[2,128,256]{1,2,0:T(8,128)(2,1)S(1)}, u32[]{:S(2)}, u32[]{:S(2)}) %collective-permute-start.2) | collective-permute-done | bytes 131104 | tf_op jit(solution)/shard_map/ppermute | solution.py:16
  54.1 0.4 fusion.137
  54.5 0.4 fusion.65
  54.9 0.4 fusion.69
  55.3 0.3 fusion.22
  55.7 0.3 fusion.24
  56.0 0.3 fusion.26
  56.3 0.3 fusion.39
  56.7 1.0 copy.179
  57.7 0.5 reshape.657
  58.2 1.4 %copy.213 = bf16[2,2,32,4,256]{4,3,2,1,0:T(4,128)(2,1)S(1)} copy(bf16[2,2,32,4,256]{2,1,0,4,3:T(2,128)(2,1)S(1)} %bitcast.218) | data formatting | bytes 524288 | tf_op jit(solution)/shard_map/all_to_all | solution.py:60
  59.8 1.9 %collective-permute-start.3 = (bf16[2,2,128,256]{3,2,1,0:T(8,128)(2,1)S(1)}, bf16[2,2,128,256]{3,2,1,0:T(8,128)(2,1)S(1)}, u32[]{:S(2)}, u32[]{:S(2)}) collective-permute-start(bf16[2,2,128,256]{3,2,1,0:T(8,128)(2,1)S(1)} %bitcast.234), channel_id=1, source_target_pairs={{0,4},{4,8},{8,12},{12,16},{16,20},{20,24},{24,28},{28,32},{32,36}... | collective-permute-start | bytes 786440 | tf_op jit(solution)/shard_map/ppermute | solution.py:16
  61.8 1.8 %fusion = (f32[128,2,8]{0,2,1:T(8,128)S(1)}, f32[2,256,128,8]{2,1,3,0:T(8,128)}) fusion(pred[128,256]{0,1:T(8,128)(4,1)S(1)} %get-tuple-element.49, bf16[128,2,8,128]{3,2,1,0:T(8,128)(2,1)S(1)} %bitcast.214, bf16[256,2,128,1]{2,1,0,3:T(2,128)(2,1)S(1)} %bitcast.226), kind=kOutput, calls=%fused_computation.8 | convolution fusion | flops 135788544 | bytes 2793472 | tf_op jit(solution)/shard_map/tgrd,kgd->tgrk/dot_general | solution.py:21
  63.6 10.4 %collective-permute-done.3 = bf16[2,2,128,256]{3,2,1,0:T(8,128)(2,1)S(1)} collective-permute-done((bf16[2,2,128,256]{3,2,1,0:T(8,128)(2,1)S(1)}, bf16[2,2,128,256]{3,2,1,0:T(8,128)(2,1)S(1)}, u32[]{:S(2)}, u32[]{:S(2)}) %collective-permute-start.3) | collective-permute-done | bytes 262176 | tf_op jit(solution)/shard_map/ppermute | solution.py:16
  74.1 1.9 %collective-permute-start.4 = (bf16[2,2,128,256]{3,2,1,0:T(8,128)(2,1)S(1)}, bf16[2,2,128,256]{3,2,1,0:T(8,128)(2,1)S(1)}, u32[]{:S(2)}, u32[]{:S(2)}) collective-permute-start(bf16[2,2,128,256]{3,2,1,0:T(8,128)(2,1)S(1)} %collective-permute-done.3), channel_id=1, source_target_pairs={{0,4},{4,8},{8,12},{12,16},{16,20},{20,24},{24,28},{28,32},{32,36}... | collective-permute-start | bytes 786440 | tf_op jit(solution)/shard_map/ppermute | solution.py:16
  76.1 0.5 fusion.1
  76.6 11.9 %collective-permute-done.4 = bf16[2,2,128,256]{3,2,1,0:T(8,128)(2,1)S(1)} collective-permute-done((bf16[2,2,128,256]{3,2,1,0:T(8,128)(2,1)S(1)}, bf16[2,2,128,256]{3,2,1,0:T(8,128)(2,1)S(1)}, u32[]{:S(2)}, u32[]{:S(2)}) %collective-permute-start.4) | collective-permute-done | bytes 262176 | tf_op jit(solution)/shard_map/ppermute | solution.py:16
  88.5 0.7 copy-done.8
  89.2 2.1 %collective-permute-start.5 = (bf16[2,2,128,256]{3,2,1,0:T(8,128)(2,1)}, bf16[2,2,128,256]{3,2,1,0:T(8,128)(2,1)S(1)}, u32[]{:S(2)}, u32[]{:S(2)}) collective-permute-start(bf16[2,2,128,256]{3,2,1,0:T(8,128)(2,1)} %copy-done.8), channel_id=1, source_target_pairs={{0,4},{4,8},{8,12},{12,16},{16,20},{20,24},{24,28},{28,32},{32,36}... | collective-permute-start | bytes 786440 | tf_op jit(solution)/shard_map/ppermute | solution.py:16
  91.3 2.4 %fusion.2 = (f32[128,2,8]{0,2,1:T(8,128)}, f32[2,256,128,8]{2,1,3,0:T(8,128)}) fusion(pred[128,256]{0,1:T(8,128)(4,1)S(1)} %get-tuple-element.47, bf16[128,2,8,128]{3,2,1,0:T(8,128)(2,1)S(1)} %bitcast.216, bf16[256,2,128,1]{2,1,0,3:T(2,128)(2,1)S(1)} %bitcast.225), kind=kOutput, calls=%fused_computation.10 | convolution fusion | flops 135788544 | bytes 2793472 | tf_op jit(solution)/shard_map/tgrd,kgd->tgrk/dot_general | solution.py:21
  93.7 10.0 %collective-permute-done.5 = bf16[2,2,128,256]{3,2,1,0:T(8,128)(2,1)S(1)} collective-permute-done((bf16[2,2,128,256]{3,2,1,0:T(8,128)(2,1)}, bf16[2,2,128,256]{3,2,1,0:T(8,128)(2,1)S(1)}, u32[]{:S(2)}, u32[]{:S(2)}) %collective-permute-start.5) | collective-permute-done | bytes 262176 | tf_op jit(solution)/shard_map/ppermute | solution.py:16
  103.8 0.5 fusion.3
  104.3 0.2 copy-done.9
  104.5 1.2 %copy-done.2 = f32[2,256,128,8]{2,1,3,0:T(8,128)S(1)} copy-done((f32[2,256,128,8]{2,1,3,0:T(8,128)S(1)}, f32[2,256,128,8]{2,1,3,0:T(8,128)}, u32[]{:S(2)}) %copy-start.2) | copy-done | bytes 2097176
  105.7 0.5 fusion.5
  106.2 0.5 fusion.7
  106.7 0.5 copy-done
  107.3 0.5 fusion.9
  107.8 0.5 fusion.11
  108.4 2.2 %fusion.20 = f32[128,2,8,128]{0,3,2,1:T(8,128)S(1)} fusion(f32[2,256,128,8]{2,1,3,0:T(8,128)} %get-tuple-element.73, f32[128,2,8]{0,2,1:T(8,128)S(1)} %get-tuple-element.43, pred[128,256]{0,1:T(8,128)(4,1)S(1)} %get-tuple-element.49, f32[128,2,8]{0,2,1:T(8,128)S(1)} %get-tuple-element.16, f32[128,2,8]{0,2,1:T(8,128)S(1)} %get-tuple-element.42, ...), kind=kOutput, calls=%fused_computation.36 | convolution fusion | flops 137363456 | bytes 3334144 | tf_op jit(solution)/shard_map/tgrk,kgd->tgrd/dot_general | solution.py:29
  110.7 0.7 fusion.18
  111.4 0.9 copy-done.1
  112.3 0.7 fusion.16
  112.9 0.9 copy-done.4
  113.8 0.7 fusion.38
  114.5 1.0 copy.180
  (63 shorter events, 1.9 us)
Async XLA Ops:
  0.6 11.1 %copy-start.7 = (bf16[2,128,256]{2,1,0:T(8,128)(2,1)S(1)}, bf16[2,128,256]{2,1,0:T(8,128)(2,1)}, u32[]{:S(2)}) copy-start(bf16[2,128,256]{2,1,0:T(8,128)(2,1)} %param.8) | copy-start | bytes 393220
  0.6 13.9 %copy-start.11 = (s32[64]{0:T(128)S(1)}, s32[64]{0:T(128)}, u32[]{:S(2)}) copy-start(s32[64]{0:T(128)} %param.10) | copy-start | bytes 772
  0.7 14.2 %copy-start.5 = (bf16[128,2048]{1,0:T(8,128)(2,1)S(1)}, bf16[128,2048]{1,0:T(8,128)(2,1)}, u32[]{:S(2)}) copy-start(bf16[128,2048]{1,0:T(8,128)(2,1)} %param.7) | copy-start | bytes 1572868
  2.9 12.1 %copy-start.6 = (bf16[128,2048]{1,0:T(8,128)(2,1)S(1)}, bf16[128,2048]{1,0:T(8,128)(2,1)}, u32[]{:S(2)}) copy-start(bf16[128,2048]{1,0:T(8,128)(2,1)} %param.6) | copy-start | bytes 1572868
  3.0 12.2 %slice-start = ((bf16[2,128,256]{2,1,0:T(8,128)(2,1)}), bf16[1,128,256]{2,1,0:T(8,128)(2,1)S(1)}, s32[]{:S(2)}) async-start(bf16[2,128,256]{2,1,0:T(8,128)(2,1)} %param.8), calls=%async_computation.1 | async-start | bytes 131072 | tf_op jit(solution)/shard_map/slice | solution.py:84
  3.0 12.3 %copy-start.10 = (s32[256]{0:T(256)S(1)}, s32[256]{0:T(256)}, u32[]{:S(2)}) copy-start(s32[256]{0:T(256)} %param.11) | copy-start | bytes 3076
  4.7 53.0 %all-to-all-start = ((bf16[4,2,16384]{2,1,0:T(2,128)(2,1)}), bf16[4,2,16384]{2,1,0:T(2,128)(2,1)S(1)}, u32[]{:S(2)}, u32[]{:S(2)}) async-start(bf16[4,2,16384]{2,1,0:T(2,128)(2,1)} %reshape.656), calls=%async_computation | async-start | bytes 524288 | tf_op jit(solution)/shard_map/all_to_all | solution.py:60
  11.9 16.3 %collective-permute-start = (bf16[2,128,256]{1,2,0:T(8,128)(2,1)S(1)}, bf16[2,128,256]{1,2,0:T(8,128)(2,1)S(1)}, u32[]{:S(2)}, u32[]{:S(2)}) collective-permute-start(bf16[2,128,256]{1,2,0:T(8,128)(2,1)S(1)} %copy.143), channel_id=1, source_target_pairs={{0,4},{4,8},{8,12},{12,16},{16,20},{20,24},{24,28},{28,32},{32,36}... | collective-permute-start | bytes 393224 | tf_op jit(solution)/shard_map/ppermute | solution.py:16
  28.2 13.0 %collective-permute-start.1 = (bf16[2,128,256]{1,2,0:T(8,128)(2,1)S(1)}, bf16[2,128,256]{1,2,0:T(8,128)(2,1)S(1)}, u32[]{:S(2)}, u32[]{:S(2)}) collective-permute-start(bf16[2,128,256]{1,2,0:T(8,128)(2,1)S(1)} %collective-permute-done), channel_id=1, source_target_pairs={{0,4},{4,8},{8,12},{12,16},{16,20},{20,24},{24,28},{28,32},{32,36}... | collective-permute-start | bytes 393224 | tf_op jit(solution)/shard_map/ppermute | solution.py:16
  41.2 12.9 %collective-permute-start.2 = (bf16[2,128,256]{1,2,0:T(8,128)(2,1)S(1)}, bf16[2,128,256]{1,2,0:T(8,128)(2,1)S(1)}, u32[]{:S(2)}, u32[]{:S(2)}) collective-permute-start(bf16[2,128,256]{1,2,0:T(8,128)(2,1)S(1)} %collective-permute-done.1), channel_id=1, source_target_pairs={{0,4},{4,8},{8,12},{12,16},{16,20},{20,24},{24,28},{28,32},{32,36}... | collective-permute-start | bytes 393224 | tf_op jit(solution)/shard_map/ppermute | solution.py:16
  59.8 14.3 %collective-permute-start.3 = (bf16[2,2,128,256]{3,2,1,0:T(8,128)(2,1)S(1)}, bf16[2,2,128,256]{3,2,1,0:T(8,128)(2,1)S(1)}, u32[]{:S(2)}, u32[]{:S(2)}) collective-permute-start(bf16[2,2,128,256]{3,2,1,0:T(8,128)(2,1)S(1)} %bitcast.234), channel_id=1, source_target_pairs={{0,4},{4,8},{8,12},{12,16},{16,20},{20,24},{24,28},{28,32},{32,36}... | collective-permute-start | bytes 786440 | tf_op jit(solution)/shard_map/ppermute | solution.py:16
  74.1 14.3 %collective-permute-start.4 = (bf16[2,2,128,256]{3,2,1,0:T(8,128)(2,1)S(1)}, bf16[2,2,128,256]{3,2,1,0:T(8,128)(2,1)S(1)}, u32[]{:S(2)}, u32[]{:S(2)}) collective-permute-start(bf16[2,2,128,256]{3,2,1,0:T(8,128)(2,1)S(1)} %collective-permute-done.3), channel_id=1, source_target_pairs={{0,4},{4,8},{8,12},{12,16},{16,20},{20,24},{24,28},{28,32},{32,36}... | collective-permute-start | bytes 786440 | tf_op jit(solution)/shard_map/ppermute | solution.py:16
  88.4 0.7 copy-start.8
  89.2 14.5 %collective-permute-start.5 = (bf16[2,2,128,256]{3,2,1,0:T(8,128)(2,1)}, bf16[2,2,128,256]{3,2,1,0:T(8,128)(2,1)S(1)}, u32[]{:S(2)}, u32[]{:S(2)}) collective-permute-start(bf16[2,2,128,256]{3,2,1,0:T(8,128)(2,1)} %copy-done.8), channel_id=1, source_target_pairs={{0,4},{4,8},{8,12},{12,16},{16,20},{20,24},{24,28},{28,32},{32,36}... | collective-permute-start | bytes 786440 | tf_op jit(solution)/shard_map/ppermute | solution.py:16
  103.8 0.7 copy-start.9
  103.8 1.9 %copy-start.2 = (f32[2,256,128,8]{2,1,3,0:T(8,128)S(1)}, f32[2,256,128,8]{2,1,3,0:T(8,128)}, u32[]{:S(2)}) copy-start(f32[2,256,128,8]{2,1,3,0:T(8,128)} %get-tuple-element.73) | copy-start | bytes 6291460
  104.3 3.5 %copy-start.3 = (f32[2,256,128,8]{2,1,3,0:T(8,128)}, f32[2,256,128,8]{2,1,3,0:T(8,128)S(1)}, u32[]{:S(2)}) copy-start(f32[2,256,128,8]{2,1,3,0:T(8,128)S(1)} %get-tuple-element.67) | copy-start | bytes 6291460
  105.7 1.6 %copy-start = (f32[2,256,128,8]{2,1,3,0:T(8,128)S(1)}, f32[2,256,128,8]{2,1,3,0:T(8,128)}, u32[]{:S(2)}) copy-start(f32[2,256,128,8]{2,1,3,0:T(8,128)} %get-tuple-element.69) | copy-start | bytes 6291460
  110.7 1.6 %copy-start.1 = (f32[2,256,128,8]{2,1,3,0:T(8,128)S(1)}, f32[2,256,128,8]{2,1,3,0:T(8,128)}, u32[]{:S(2)}) copy-start(f32[2,256,128,8]{2,1,3,0:T(8,128)} %get-tuple-element.69) | copy-start | bytes 6291460
  112.3 1.6 %copy-start.4 = (f32[2,256,128,8]{2,1,3,0:T(8,128)S(1)}, f32[2,256,128,8]{2,1,3,0:T(8,128)}, u32[]{:S(2)}) copy-start(f32[2,256,128,8]{2,1,3,0:T(8,128)} %copy-done.3) | copy-start | bytes 6291460
where the time goes:
time: 116 us
  waiting for transfers between devices  65.4 us (56%)
  starting transfers between devices  19.4 us (17%)
  local copies, waits for them, and re-layouts  13.6 us (12%)
  matrix products  12.1 us (10%)
  other arithmetic  3.76 us (3%)
  between operations  1.21 us (1%)
    ppermute x6, waiting for transfers between devices, shifted(): lax.ppermute(value, axis, [(source, source + steps) for source in range(i...  65.4 us
    ppermute x6, starting transfers between devices, shifted(): lax.ppermute(value, axis, [(source, source + steps) for source in range(i...  12.3 us
    unnamed x32, local copies, waits for them, and re-layouts  11.3 us
    all_to_all x1, starting transfers between devices, per_device(): lax.all_to_all(image_pairs, 'tp', split_axis=3, concat_axis=2, tiled=True)  7.09 us
    dot_general x8, matrix products, absorb(): jnp.einsum('tgrd,kgd->tgrk', queries, key_block, preferred_element_type=j...  6.6 us
    dot_general x8, matrix products, absorb(): jnp.einsum('tgrk,kgd->tgrd', weights.astype(jnp.bfloat16), value_block, p...  5.53 us
    reduce_sum x6, other arithmetic, absorb(): running_sum = running_sum * factor + jnp.sum(weights, axis=-1)  2.91 us
  transfers between devices with their start and end apart: 7, of which 6 were waited for; matrix products, arithmetic and copies ran while one was open for 9% of the time, Pallas kernels for 0%

commit v1 on v0

v1 whole, which is shorter than its diff:
```python
import functools
import math
import jax
import jax.numpy as jnp
from jax import lax
from jax.experimental import pallas as pl
from jax.experimental.pallas import tpu as pltpu
from jax.sharding import PartitionSpec as P

HEAD_DIM = 128
ROW = 4
OWN = 4
TEXT, NEAR, FAR = 0, 5, 10
HIDDEN = -1e30
LOWEST = -1e29
EXPONENT = math.log2(math.e) / math.sqrt(HEAD_DIM)
MESH = pl.DeviceIdType.MESH

ARRIVALS = (
    (TEXT, (1, 0, 1, 2), (0, 1, 1, 0)),
    (FAR, (3, 3, 0, 0), (1, 1, -1, -1)),
    (FAR, (2, 2, 1, 1), (1, -3, -1, -1)),
    (NEAR, (1, 0, 1, 2), (0, 1, 1, 0)),
    (TEXT, (2, 2, 3, 1), (0, -1, -1, 0)),
    (NEAR, (2, 2, 3, 1), (0, -1, -1, 0)),
    (FAR, (0, 0, 3, 3), (0, -1, -3, 0)),
    (TEXT, (3, 3, 0, 0), (0, -1, 1, 0)),
    (NEAR, (3, 3, 0, 0), (0, -1, 1, 0)),
    (FAR, (1, 1, 2, 2), (0, 3, 1, 0)),
)
FAR_STEP = (3, 2, 2, 1)


def pick(place, values):
    result = jnp.int32(values[-1])
    for index, value in enumerate(values[:-1]):
        result = jnp.where(place == index, value, result)
    return result


def attend(queries, chunks, bias, tops, totals, sums, kind, chunk, first):
    for group in range(2):
        columns = slice(group * HEAD_DIM, (group + 1) * HEAD_DIM)
        keys = chunks[chunk, 0, :, :, :, columns].reshape(HEAD_DIM, HEAD_DIM)
        values = chunks[chunk, 1, :, :, :, columns].reshape(HEAD_DIM, HEAD_DIM)
        heads = [queries[kind, :, h * HEAD_DIM : (h + 1) * HEAD_DIM] for h in range(group * 8, group * 8 + 8)]
        stacked = jnp.concatenate(heads, axis=0)
        scores = lax.dot_general(stacked, keys, (((1,), (1,)), ((), ())), preferred_element_type=jnp.float32)
        scores = (scores.reshape(8, 128, 128) + bias[...][None]).reshape(1024, 128)
        top = jnp.max(scores, axis=1, keepdims=True)
        if first:
            new_top = jnp.broadcast_to(jnp.maximum(top, LOWEST), (1024, 128))
            weights = jnp.exp2((scores - new_top) * EXPONENT)
            total = weights
            weighted = jnp.dot(weights.astype(jnp.bfloat16), values, preferred_element_type=jnp.float32)
        else:
            old_top = tops[kind, group]
            new_top = jnp.maximum(old_top, top)
            weights = jnp.exp2((scores - new_top) * EXPONENT)
            factor = jnp.exp2((old_top - new_top) * EXPONENT)
            total = totals[kind, group] * factor + weights
            weighted = sums[kind, group] * factor + jnp.dot(
                weights.astype(jnp.bfloat16), values, preferred_element_type=jnp.float32
            )
        tops[kind, group] = new_top
        totals[kind, group] = total
        sums[kind, group] = weighted


def finish(staged, totals, sums, kind):
    for head in range(16):
        rows = slice((head % 8) * 128, (head % 8 + 1) * 128)
        total = jnp.sum(totals[kind, head // 8, rows, :], axis=1, keepdims=True)
        positive = total > 0.0
        inverse = jnp.where(positive, 1.0 / jnp.where(positive, total, 1.0), 0.0)
        result = sums[kind, head // 8, rows, :] * inverse
        staged[kind, :, head * HEAD_DIM : (head + 1) * HEAD_DIM] = result.astype(jnp.bfloat16)


def kernel(
    blocks,
    self_queries,
    cross_queries,
    text,
    images,
    lengths,
    image_places,
    self_out,
    cross_out,
    queries,
    chunks,
    staged,
    bias,
    begins,
    tops,
    totals,
    sums,
    local_sems,
    send_sems,
    recv_sems,
):
    block = lax.axis_index("ctx")
    lane = lax.axis_index("tp")
    place = lax.rem(block, ROW)
    core = lax.rem(lane, 2)
    other_lane = lane + 1 - 2 * core
    far_lane = lax.rem(lane + 2, 4)
    other_far_lane = lax.rem(other_lane + 2, 4)

    def at(step, to_lane):
        return (lax.rem(block + step + blocks, blocks), to_lane)

    barrier = pltpu.get_barrier_semaphore()

    def greet(step, to_lane):
        pl.semaphore_signal(barrier, inc=1, device_id=at(step, to_lane), device_id_type=MESH)

    greet(0, other_lane)

    @pl.when(place >= 1)
    def _():
        greet(-1, lane)

    @pl.when(place <= 2)
    def _():
        greet(1, lane)
        greet(-3, lane)

    @pl.when(place >= 2)
    def _():
        greet(3, lane)

    @pl.when(place == 0)
    def _():
        greet(-1, far_lane)
        greet(-2, far_lane)

    @pl.when(place == 3)
    def _():
        greet(-3, far_lane)
        greet(-2, far_lane)

    def columns(of_lane):
        return images.at[:, :, :, pl.ds(pl.multiple_of(of_lane * 256, 256), 256)]

    loads = [
        pltpu.make_async_copy(text, chunks.at[TEXT + OWN], local_sems.at[0]),
        pltpu.make_async_copy(columns(lane), chunks.at[NEAR + OWN, :, :, core], local_sems.at[1]),
        pltpu.make_async_copy(columns(far_lane), chunks.at[FAR + OWN, :, :, core], local_sems.at[2]),
        pltpu.make_async_copy(self_queries, queries.at[0], local_sems.at[3]),
        pltpu.make_async_copy(cross_queries, queries.at[1], local_sems.at[4]),
    ]
    for load in loads:
        load.start()

    row_index = lax.broadcasted_iota(jnp.int32, (64, 64), 0)
    column_index = lax.broadcasted_iota(jnp.int32, (64, 64), 1)
    spread = jnp.broadcast_to(lengths[...].astype(jnp.float32), (64, 64))
    starts = jnp.sum(jnp.where(column_index < row_index, spread, 0.0), axis=1, keepdims=True)
    starts = jnp.sum(jnp.where(column_index == row_index, starts, 0.0), axis=0, keepdims=True)
    tokens = block * 128 + lax.broadcasted_iota(jnp.int32, (128, 64), 0)
    begin = jnp.max(jnp.where(starts <= tokens.astype(jnp.float32), starts, 0.0), axis=1, keepdims=True)
    begins[...] = jnp.broadcast_to(begin, (128, 128)).astype(jnp.int32)

    def mask(positions):
        token = block * 128 + lax.broadcasted_iota(jnp.int32, (128, 128), 0)
        seen = (positions >= begins[...]) & (positions <= token)
        bias[...] = jnp.where(seen, 0.0, HIDDEN)

    def take(group, source, chunk, first):
        index = lax.broadcasted_iota(jnp.int32, (128, 128), 1)
        if group == TEXT:
            mask(source * 128 + index)
        else:
            slot = jnp.maximum(source, 0) * 2
            left = jnp.where(source >= 0, image_places[slot], -1)
            right = jnp.where(source >= 0, image_places[slot + 1], -1)
            mask(jnp.where(index < 64, left, right))
        kind = 0 if group == TEXT else 1
        attend(queries, chunks, bias, tops, totals, sums, kind, chunk, first)

    def send(source, target, sem, receive, device):
        return pltpu.make_async_remote_copy(
            src_ref=source,
            dst_ref=target,
            send_sem=send_sems.at[sem],
            recv_sem=recv_sems.at[receive],
            device_id=device,
            device_id_type=MESH,
        )

    def own(group, sem, step):
        return send(chunks.at[group + OWN], chunks.at[group + place], sem, group + place, at(step, lane))

    pl.semaphore_wait(barrier, pick(place, (3, 6, 6, 4)))
    swap_near = send(columns(other_lane), chunks.at[NEAR + OWN, :, :, core], 0, NEAR + OWN, at(0, other_lane))
    swap_far = send(columns(other_far_lane), chunks.at[FAR + OWN, :, :, core], 1, FAR + OWN, at(0, other_lane))
    swap_far.start()
    swap_near.start()

    def own_to_row(group, sem):
        ahead, across = own(group, sem, 1), own(group, sem + 1, 3)

        @pl.when(place <= 2)
        def _():
            ahead.start()

        @pl.when(place >= 1)
        def _():
            across.start()

    def own_to_row_wait(group, sem):
        ahead, across = own(group, sem, 1), own(group, sem + 1, 3)

        @pl.when(place <= 2)
        def _():
            ahead.wait_send()

        @pl.when(place >= 1)
        def _():
            across.wait_send()

    loads[0].wait()
    own_to_row(TEXT, 2)
    loads[2].wait()
    swap_far.wait_recv()
    to_far = send(
        chunks.at[FAR + OWN], chunks.at[FAR + place], 4, FAR + place, at(pick(place, FAR_STEP), far_lane)
    )
    to_far.start()
    loads[1].wait()
    swap_near.wait_recv()
    own_to_row(NEAR, 5)
    loads[3].wait()
    take(TEXT, block, TEXT + OWN, True)
    loads[4].wait()
    take(NEAR, block, NEAR + OWN, True)

    forwards = []
    self_left = 3
    store_self = pltpu.make_async_copy(staged.at[0], self_out, local_sems.at[5])
    for number, (group, sources, steps) in enumerate(ARRIVALS):
        source = pick(place, sources)
        chunk = group + source
        step = pick(place, steps)
        forward = send(chunks.at[chunk], chunks.at[chunk], 7 + number, chunk, at(step, lane))
        forward.wait_recv()

        @pl.when(step != 0)
        def _(forward=forward):
            forward.start()

        forwards.append((step, forward))
        take(group, block - place + source - jnp.where(source > place, ROW, 0), chunk, False)
        if group == TEXT:
            self_left -= 1
            if self_left == 0:
                finish(staged, totals, sums, 0)
                store_self.start()
    finish(staged, totals, sums, 1)
    store_cross = pltpu.make_async_copy(staged.at[1], cross_out, local_sems.at[6])
    store_cross.start()
    swap_near.wait_send()
    swap_far.wait_send()
    to_far.wait_send()
    own_to_row_wait(TEXT, 2)
    own_to_row_wait(NEAR, 5)
    for step, forward in forwards:

        @pl.when(step != 0)
        def _(forward=forward):
            forward.wait_send()

    store_self.wait()
    store_cross.wait()


def per_device(self_queries, cross_queries, text_pairs, image_pairs, doc_lengths, image_places):
    anywhere = pl.BlockSpec(memory_space=pl.ANY)
    result = jax.ShapeDtypeStruct(self_queries.shape, jnp.bfloat16)
    state = pltpu.VMEM((2, 2, 1024, HEAD_DIM), jnp.float32)
    return pl.pallas_call(
        functools.partial(kernel, lax.axis_size("ctx")),
        out_shape=(result, result),
        in_specs=[
            anywhere,
            anywhere,
            anywhere,
            anywhere,
            pl.BlockSpec(memory_space=pltpu.VMEM),
            pl.BlockSpec(memory_space=pltpu.SMEM),
        ],
        out_specs=(anywhere, anywhere),
        scratch_shapes=[
            pltpu.VMEM((2, 128, 2048), jnp.bfloat16),
            pltpu.VMEM((15, 2, 2, 2, 32, 256), jnp.bfloat16),
            pltpu.VMEM((2, 128, 2048), jnp.bfloat16),
            pltpu.VMEM((128, 128), jnp.float32),
            pltpu.VMEM((128, 128), jnp.int32),
            state,
            state,
            state,
            pltpu.SemaphoreType.DMA((7,)),
            pltpu.SemaphoreType.DMA((7 + len(ARRIVALS),)),
            pltpu.SemaphoreType.DMA((15,)),
        ],
        compiler_params=pltpu.CompilerParams(
            collective_id=0, has_side_effects=True, vmem_limit_bytes=40 << 20
        ),
    )(
        self_queries,
        cross_queries,
        text_pairs.reshape(2, 2, 2, 32, 256),
        image_pairs,
        doc_lengths.reshape(1, 64),
        image_places,
    )


def solution(mesh):
    placed = (
        P("ctx", "tp"),
        P("ctx", "tp"),
        P(None, "ctx", "tp"),
        P(None, "ctx", "tp", None),
        P(),
        P(),
    )
    return jax.shard_map(
        per_device,
        mesh=mesh,
        in_specs=placed,
        out_specs=(P("ctx", "tp"), P("ctx", "tp")),
        check_vma=False,
    )
```

time: 116 us -> 64.4 us (0.56)
  the two profiles are of different devices: /device:TPU:256 before, /device:TPU:1 now
where the time goes in v1:
time: 64.4 us; the launch traced here: 64.1 us
  Pallas kernels  57.2 us (89%)
  local copies, waits for them, and re-layouts  6.19 us (10%)
  between operations  0.66 us (1%)
    pallas_call x1, Pallas kernels, per_device(): pl.pallas_call(functools.partial(kernel, lax.axis_size('ctx')), out_shape...  57.2 us
    unnamed x14, local copies, waits for them, and re-layouts  6.19 us

profile of v1, /device:TPU:1, one launch (start us, length us, event | category | flops | bytes accessed | tf_op | source)
XLA Modules:
  0.0 64.1 jit_solution(14213347887120581505)
XLA Ops:
  0.6 0.0 copy-start.4
  0.6 0.0 copy-start.5
  0.7 0.7 %copy-done.4 = s32[256]{0:T(256)S(1)} copy-done((s32[256]{0:T(256)S(1)}, s32[256]{0:T(256)}, u32[]{:S(2)}) %copy-start.4) | copy-done | bytes 1048
  1.3 0.0 copy-done.5
  1.3 0.0 copy-start
  1.3 1.0 %copy-done = bf16[128,2048]{1,0:T(8,128)(2,1)S(1)} copy-done((bf16[128,2048]{1,0:T(8,128)(2,1)S(1)}, bf16[128,2048]{1,0:T(8,128)(2,1)}, u32[]{:S(2)}) %copy-start) | copy-done | bytes 524312
  2.4 0.0 copy-start.1
  2.4 1.0 %copy-done.1 = bf16[128,2048]{1,0:T(8,128)(2,1)S(1)} copy-done((bf16[128,2048]{1,0:T(8,128)(2,1)S(1)}, bf16[128,2048]{1,0:T(8,128)(2,1)}, u32[]{:S(2)}) %copy-start.1) | copy-done | bytes 524312
  3.4 0.0 copy-start.2
  3.4 0.9 %copy-done.2 = bf16[2,2,32,1024]{3,2,1,0:T(8,128)(2,1)S(1)} copy-done((bf16[2,2,32,1024]{3,2,1,0:T(8,128)(2,1)S(1)}, bf16[2,2,32,1024]{3,2,1,0:T(8,128)(2,1)}, u32[]{:S(2)}) %copy-start.2) | copy-done | bytes 262168
  4.3 0.0 copy-start.3
  4.4 0.9 %copy-done.3 = bf16[2,128,256]{2,1,0:T(8,128)(2,1)S(1)} copy-done((bf16[2,128,256]{2,1,0:T(8,128)(2,1)S(1)}, bf16[2,128,256]{2,1,0:T(8,128)(2,1)}, u32[]{:S(2)}) %copy-start.3) | copy-done | bytes 131096
  5.3 57.2 %shard_map.77 = (bf16[128,2048]{1,0:T(8,128)(2,1)S(1)}, bf16[128,2048]{1,0:T(8,128)(2,1)S(1)}) custom-call(bf16[128,2048]{1,0:T(8,128)(2,1)S(1)} %copy-done, bf16[128,2048]{1,0:T(8,128)(2,1)S(1)} %copy-done.1, bf16[2,2,2,32,256]{4,3,2,1,0:T(8,128)(2,1)S(1)} %bitcast.2, bf16[2,2,32,1024]{3,2,1,0:T(8,128)(2,1)S(1)} %copy-done.2, s32[1,64]{1,0:T(1,128)S(1)} %bitcast.3, ...), custom_call_target="tpu_custom_call" | custom-call | tf_op jit(solution)/shard_map/pallas_call | solution.py:282
  62.5 0.8 %copy.10 = bf16[128,2048]{1,0:T(8,128)(2,1)} copy(bf16[128,2048]{1,0:T(8,128)(2,1)S(1)} %get-tuple-element.4) | data formatting | bytes 1048576
  63.3 0.8 %copy.11 = bf16[128,2048]{1,0:T(8,128)(2,1)} copy(bf16[128,2048]{1,0:T(8,128)(2,1)S(1)} %get-tuple-element.5) | data formatting | bytes 1048576
Async XLA Ops:
  0.6 0.7 %copy-start.4 = (s32[256]{0:T(256)S(1)}, s32[256]{0:T(256)}, u32[]{:S(2)}) copy-start(s32[256]{0:T(256)} %image_places.1) | copy-start | bytes 3076
  0.6 0.7 %copy-start.5 = (s32[64]{0:T(128)S(1)}, s32[64]{0:T(128)}, u32[]{:S(2)}) copy-start(s32[64]{0:T(128)} %param.10) | copy-start | bytes 772
  1.3 1.0 %copy-start = (bf16[128,2048]{1,0:T(8,128)(2,1)S(1)}, bf16[128,2048]{1,0:T(8,128)(2,1)}, u32[]{:S(2)}) copy-start(bf16[128,2048]{1,0:T(8,128)(2,1)} %self_queries.1) | copy-start | bytes 1572868
  2.4 1.0 %copy-start.1 = (bf16[128,2048]{1,0:T(8,128)(2,1)S(1)}, bf16[128,2048]{1,0:T(8,128)(2,1)}, u32[]{:S(2)}) copy-start(bf16[128,2048]{1,0:T(8,128)(2,1)} %cross_queries.1) | copy-start | bytes 1572868
  3.4 0.9 %copy-start.2 = (bf16[2,2,32,1024]{3,2,1,0:T(8,128)(2,1)S(1)}, bf16[2,2,32,1024]{3,2,1,0:T(8,128)(2,1)}, u32[]{:S(2)}) copy-start(bf16[2,2,32,1024]{3,2,1,0:T(8,128)(2,1)} %images.1) | copy-start | bytes 786436
  4.3 0.9 %copy-start.3 = (bf16[2,128,256]{2,1,0:T(8,128)(2,1)S(1)}, bf16[2,128,256]{2,1,0:T(8,128)(2,1)}, u32[]{:S(2)}) copy-start(bf16[2,128,256]{2,1,0:T(8,128)(2,1)} %param.8) | copy-start | bytes 393220

commit v2 on v1

--- a/solution.py
+++ b/solution.py
@@ -16,19 +16,48 @@
 EXPONENT = math.log2(math.e) / math.sqrt(HEAD_DIM)
 MESH = pl.DeviceIdType.MESH
 
-ARRIVALS = (
-    (TEXT, (1, 0, 1, 2), (0, 1, 1, 0)),
-    (FAR, (3, 3, 0, 0), (1, 1, -1, -1)),
-    (FAR, (2, 2, 1, 1), (1, -3, -1, -1)),
-    (NEAR, (1, 0, 1, 2), (0, 1, 1, 0)),
-    (TEXT, (2, 2, 3, 1), (0, -1, -1, 0)),
-    (NEAR, (2, 2, 3, 1), (0, -1, -1, 0)),
-    (FAR, (0, 0, 3, 3), (0, -1, -3, 0)),
-    (TEXT, (3, 3, 0, 0), (0, -1, 1, 0)),
-    (NEAR, (3, 3, 0, 0), (0, -1, 1, 0)),
-    (FAR, (1, 1, 2, 2), (0, 3, 1, 0)),
+ORDER = (
+    ("G3a", "G2a", "T1a", "I1a", "T2a", "G2b", "T1b", "I1b", "T2b", "G3b", "I2b", "G0a", "I3a", "T3b", "I3b", "T3a", "I2a", "G0b", "G1a", "G1b"),
+    ("T0b", "T2a", "I0b", "T0a", "I0a", "T2b", "I2a", "I2b", "T3b", "G3a", "T3a", "G2a", "I3a", "G2b", "I3b", "G3b", "G1a", "G0a", "G0b", "G1b"),
+    ("T1b", "T1a", "T3b", "T3a", "I3a", "I1a", "T0b", "I3b", "G0a", "I1b", "I0a", "G1a", "I0b", "T0a", "G0b", "G1b", "G3a", "G2a", "G2b", "G3b"),
+    ("G0a", "G1a", "I2a", "I2b", "G0b", "T1a", "G1b", "I0a", "T1b", "T2b", "T0a", "G3a", "G2a", "I0b", "I1b", "I1a", "T0b", "T2a", "G2b", "G3b"),
 )
+CLASSES = {"T": TEXT, "I": NEAR, "G": FAR}
+PARTS = {"a": 0, "b": 1}
+FAR_ON = ((0, -1, -1, -1), (0, 3, -1, -1), (1, -3, 1, 0), (1, 1, -3, 0))
+
+
+def onward(group, source, place):
+    if group == FAR:
+        return FAR_ON[source][place]
+    if source < place:
+        return 1 if place < ROW - 1 else 0
+    return -1 if place > 0 else 0
+
+
+def plan():
+    orders = [[(CLASSES[word[0]], int(word[1]), PARTS[word[2]]) for word in order] for order in ORDER]
+    whole = []
+    for order in orders:
+        seen, done = set(), []
+        for number, (group, source, _) in enumerate(order):
+            if (group, source) in seen:
+                done.append((number, group, source))
+            seen.add((group, source))
+        whole.append(done)
+    ready = [[] for _ in orders[0]]
+    for entry in zip(*whole):
+        ready[max(number for number, _, _ in entry)].append(
+            (tuple(group for _, group, _ in entry), tuple(source for _, _, source in entry))
+        )
+    for number, entry in enumerate(zip(*orders)):
+        groups, sources, parts = (tuple(column) for column in zip(*entry))
+        steps = tuple(onward(groups[place], sources[place], place) for place in range(ROW))
+        yield groups, sources, parts, steps, ready[number]
+
+
 FAR_STEP = (3, 2, 2, 1)
+FAR_STEP_LAST = (3, 2, 0, 0)
 
 
 def pick(place, values):
@@ -83,10 +112,12 @@
     cross_queries,
     text,
     images,
+    lengths_hbm,
+    places_hbm,
+    self_out,
+    cross_out,
     lengths,
     image_places,
-    self_out,
-    cross_out,
     queries,
     chunks,
     staged,
@@ -110,6 +141,9 @@
     def at(step, to_lane):
         return (lax.rem(block + step + blocks, blocks), to_lane)
 
+    first_row = block < ROW
+    last_row = block >= blocks - ROW
+
     barrier = pltpu.get_barrier_semaphore()
 
     def greet(step, to_lane):
@@ -124,13 +158,20 @@
     @pl.when(place <= 2)
     def _():
         greet(1, lane)
+
+    @pl.when((place <= 2) & ~first_row)
+    def _():
         greet(-3, lane)
 
-    @pl.when(place >= 2)
+    @pl.when((place >= 2) & ~last_row)
     def _():
         greet(3, lane)
 
-    @pl.when(place == 0)
+    @pl.when((place >= 2) & last_row)
+    def _():
+        greet(0, far_lane)
+
+    @pl.when((place == 0) & ~first_row)
     def _():
         greet(-1, far_lane)
         greet(-2, far_lane)
@@ -149,9 +190,14 @@
         pltpu.make_async_copy(columns(far_lane), chunks.at[FAR + OWN, :, :, core], local_sems.at[2]),
         pltpu.make_async_copy(self_queries, queries.at[0], local_sems.at[3]),
         pltpu.make_async_copy(cross_queries, queries.at[1], local_sems.at[4]),
+        pltpu.make_async_copy(lengths_hbm, lengths, local_sems.at[7]),
+        pltpu.make_async_copy(places_hbm, image_places, local_sems.at[8]),
     ]
     for load in loads:
         load.start()
+
+    loads[5].wait()
+    loads[6].wait()
 
     row_index = lax.broadcasted_iota(jnp.int32, (64, 64), 0)
     column_index = lax.broadcasted_iota(jnp.int32, (64, 64), 1)
@@ -169,14 +215,11 @@
 
     def take(group, source, chunk, first):
         index = lax.broadcasted_iota(jnp.int32, (128, 128), 1)
-        if group == TEXT:
-            mask(source * 128 + index)
-        else:
-            slot = jnp.maximum(source, 0) * 2
-            left = jnp.where(source >= 0, image_places[slot], -1)
-            right = jnp.where(source >= 0, image_places[slot + 1], -1)
-            mask(jnp.where(index < 64, left, right))
-        kind = 0 if group == TEXT else 1
+        slot = jnp.maximum(source, 0) * 2
+        left = jnp.where(source >= 0, image_places[slot], -1)
+        right = jnp.where(source >= 0, image_places[slot + 1], -1)
+        mask(jnp.where(group == TEXT, source * 128 + index, jnp.where(index < 64, left, right)))
+        kind = jnp.where(group == TEXT, 0, 1)
         attend(queries, chunks, bias, tops, totals, sums, kind, chunk, first)
 
     def send(source, target, sem, receive, device):
@@ -184,92 +227,112 @@
             src_ref=source,
             dst_ref=target,
             send_sem=send_sems.at[sem],
-            recv_sem=recv_sems.at[receive],
+            recv_sem=receive,
             device_id=device,
             device_id_type=MESH,
         )
 
-    def own(group, sem, step):
-        return send(chunks.at[group + OWN], chunks.at[group + place], sem, group + place, at(step, lane))
-
-    pl.semaphore_wait(barrier, pick(place, (3, 6, 6, 4)))
-    swap_near = send(columns(other_lane), chunks.at[NEAR + OWN, :, :, core], 0, NEAR + OWN, at(0, other_lane))
-    swap_far = send(columns(other_far_lane), chunks.at[FAR + OWN, :, :, core], 1, FAR + OWN, at(0, other_lane))
+    def sources_of_own(group, sem):
+        for part in range(2):
+            for kind, (step, goes) in enumerate(((1, place <= 2), (3, (place >= 1) & ~last_row))):
+                yield goes, send(
+                    chunks.at[group + OWN, part],
+                    chunks.at[group + place, part],
+                    sem + 2 * part + kind,
+                    recv_sems.at[group + place, part],
+                    at(step, lane),
+                )
+
+    expected = pick(place, (3, 6, 6, 4)) - jnp.where(last_row & (place >= 1), 1, 0)
+    expected = expected - jnp.where(first_row & ((place == 1) | (place == 2)), 1, 0)
+    pl.semaphore_wait(barrier, expected)
+    own_near, own_far = NEAR + OWN, FAR + OWN
+    swap_far = send(
+        columns(other_far_lane), chunks.at[own_far, :, :, core], 0, recv_sems.at[own_far, 0], at(0, other_lane)
+    )
+    swap_near = send(
+        columns(other_lane), chunks.at[own_near, :, :, core], 1, recv_sems.at[own_near, 0], at(0, other_lane)
+    )
     swap_far.start()
     swap_near.start()
 
-    def own_to_row(group, sem):
-        ahead, across = own(group, sem, 1), own(group, sem + 1, 3)
-
-        @pl.when(place <= 2)
-        def _():
-            ahead.start()
-
-        @pl.when(place >= 1)
-        def _():
-            across.start()
-
-    def own_to_row_wait(group, sem):
-        ahead, across = own(group, sem, 1), own(group, sem + 1, 3)
-
-        @pl.when(place <= 2)
-        def _():
-            ahead.wait_send()
-
-        @pl.when(place >= 1)
-        def _():
-            across.wait_send()
+    def start(copies):
+        for goes, copy in copies:
+
+            @pl.when(goes)
+            def _(copy=copy):
+                copy.start()
 
     loads[0].wait()
-    own_to_row(TEXT, 2)
+    sent = list(sources_of_own(TEXT, 2))
+    start(sent)
     loads[2].wait()
     swap_far.wait_recv()
-    to_far = send(
-        chunks.at[FAR + OWN], chunks.at[FAR + place], 4, FAR + place, at(pick(place, FAR_STEP), far_lane)
-    )
-    to_far.start()
+    far_step = jnp.where(last_row, pick(place, FAR_STEP_LAST), pick(place, FAR_STEP))
+    to_far = [
+        send(
+            chunks.at[own_far, part],
+            chunks.at[FAR + place, part],
+            6 + part,
+            recv_sems.at[FAR + place, part],
+            at(far_step, far_lane),
+        )
+        for part in range(2)
+    ]
+    for copy in to_far:
+        copy.start()
     loads[1].wait()
     swap_near.wait_recv()
-    own_to_row(NEAR, 5)
+    sent_near = list(sources_of_own(NEAR, 8))
+    start(sent_near)
+    sent += sent_near
     loads[3].wait()
     take(TEXT, block, TEXT + OWN, True)
     loads[4].wait()
     take(NEAR, block, NEAR + OWN, True)
 
-    forwards = []
-    self_left = 3
     store_self = pltpu.make_async_copy(staged.at[0], self_out, local_sems.at[5])
-    for number, (group, sources, steps) in enumerate(ARRIVALS):
-        source = pick(place, sources)
+    for number, (groups, sources, parts, steps, ready) in enumerate(plan()):
+        group, source, part, step = (pick(place, table) for table in (groups, sources, parts, steps))
         chunk = group + source
-        step = pick(place, steps)
-        forward = send(chunks.at[chunk], chunks.at[chunk], 7 + number, chunk, at(step, lane))
-        forward.wait_recv()
-
-        @pl.when(step != 0)
+        origin = block - place + source - jnp.where(source > place, ROW, 0)
+        forward = send(
+            chunks.at[chunk, part], chunks.at[chunk, part], 12 + number, recv_sems.at[chunk, part], at(step, lane)
+        )
+        goes = (origin >= 0) & (step != 0) & ~((step == 3) & last_row)
+        if number == len(ORDER[0]) - 1:
+            finish(staged, totals, sums, 0)
+            store_self.start()
+
+        @pl.when(origin >= 0)
+        def _(forward=forward):
+            forward.wait_recv()
+
+        @pl.when(goes)
         def _(forward=forward):
             forward.start()
 
-        forwards.append((step, forward))
-        take(group, block - place + source - jnp.where(source > place, ROW, 0), chunk, False)
-        if group == TEXT:
-            self_left -= 1
-            if self_left == 0:
-                finish(staged, totals, sums, 0)
-                store_self.start()
+        sent.append((goes, forward))
+        for whole_groups, whole_sources in ready:
+            group, source = pick(place, whole_groups), pick(place, whole_sources)
+            origin = block - place + source - jnp.where(source > place, ROW, 0)
+
+            @pl.when(origin >= 0)
+            def _(group=group, source=source, origin=origin):
+                take(group, origin, group + source, False)
+
     finish(staged, totals, sums, 1)
     store_cross = pltpu.make_async_copy(staged.at[1], cross_out, local_sems.at[6])
     store_cross.start()
     swap_near.wait_send()
     swap_far.wait_send()
-    to_far.wait_send()
-    own_to_row_wait(TEXT, 2)
-    own_to_row_wait(NEAR, 5)
-    for step, forward in forwards:
-
-        @pl.when(step != 0)
-        def _(forward=forward):
-            forward.wait_send()
+    for copy in to_far:
+        copy.wait_send()
+    for goes, copy in sent:
+
+        @pl.when(goes)
+        def _(copy=copy):
+            copy.wait_send()
 
     store_self.wait()
     store_cross.wait()
@@ -282,16 +345,11 @@
     return pl.pallas_call(
         functools.partial(kernel, lax.axis_size("ctx")),
         out_shape=(result, result),
-        in_specs=[
-            anywhere,
-            anywhere,
-            anywhere,
-            anywhere,
-            pl.BlockSpec(memory_space=pltpu.VMEM),
-            pl.BlockSpec(memory_space=pltpu.SMEM),
-        ],
+        in_specs=[anywhere] * 6,
         out_specs=(anywhere, anywhere),
         scratch_shapes=[
+            pltpu.VMEM((1, 64), jnp.int32),
+            pltpu.SMEM((256,), jnp.int32),
             pltpu.VMEM((2, 128, 2048), jnp.bfloat16),
             pltpu.VMEM((15, 2, 2, 2, 32, 256), jnp.bfloat16),
             pltpu.VMEM((2, 128, 2048), jnp.bfloat16),
@@ -300,12 +358,12 @@
             state,
             state,
             state,
-            pltpu.SemaphoreType.DMA((7,)),
-            pltpu.SemaphoreType.DMA((7 + len(ARRIVALS),)),
-            pltpu.SemaphoreType.DMA((15,)),
+            pltpu.SemaphoreType.DMA((9,)),
+            pltpu.SemaphoreType.DMA((12 + len(ORDER[0]),)),
+            pltpu.SemaphoreType.DMA((15, 2)),
         ],
         compiler_params=pltpu.CompilerParams(
-            collective_id=0, has_side_effects=True, vmem_limit_bytes=40 << 20
+            collective_id=0, has_side_effects=True, vmem_limit_bytes=60 << 20
         ),
     )(
         self_queries,

time: 64.4 us -> 43 us (0.67)
  the two profiles are of different devices: /device:TPU:1 before, /device:TPU:230 now
where the time goes in v2:
time: 43 us; the launch traced here: 42.9 us
  Pallas kernels  39.5 us (92%)
  local copies, waits for them, and re-layouts  2.74 us (6%)
  between operations  0.65 us (2%)
    pallas_call x1, Pallas kernels, per_device(): pl.pallas_call(functools.partial(kernel, lax.axis_size('ctx')), out_shape...  39.5 us
    unnamed x4, local copies, waits for them, and re-layouts  2.74 us

profile of v2, /device:TPU:230, one launch (start us, length us, event | category | flops | bytes accessed | tf_op | source)
XLA Modules:
  0.0 42.9 jit_solution(16372169094744532709)
XLA Ops:
  0.6 39.5 %shard_map.77 = (bf16[128,2048]{1,0:T(8,128)(2,1)}, bf16[128,2048]{1,0:T(8,128)(2,1)}) custom-call(bf16[128,2048]{1,0:T(8,128)(2,1)} %self_queries.1, bf16[128,2048]{1,0:T(8,128)(2,1)} %cross_queries.1, bf16[2,2,2,32,256]{4,3,2,1,0:T(8,128)(2,1)} %bitcast.2, bf16[2,2,32,1024]{3,2,1,0:T(8,128)(2,1)} %images.1, s32[1,64]{1,0:T(1,128)} %bitcast.3, s32[256]{0:T(256)} %places_hbm.1), custom_call_target="tpu_custom_call" | custom-call | tf_op jit(solution)/shard_map/pallas_call | solution.py:345
  40.1 0.0 copy-start
  40.1 1.9 %copy.10 = bf16[128,2048]{1,0:T(8,128)(2,1)} copy(bf16[128,2048]{1,0:T(8,128)(2,1)} %get-tuple-element.4) | data formatting | bytes 1048576
  42.1 0.0 copy-done
  42.1 0.8 %copy.11 = bf16[128,2048]{1,0:T(8,128)(2,1)} copy(bf16[128,2048]{1,0:T(8,128)(2,1)S(1)} %copy-done) | data formatting | bytes 1048576
Async XLA Ops:
  40.1 2.0 %copy-start = (bf16[128,2048]{1,0:T(8,128)(2,1)S(1)}, bf16[128,2048]{1,0:T(8,128)(2,1)}, u32[]{:S(2)}) copy-start(bf16[128,2048]{1,0:T(8,128)(2,1)} %get-tuple-element.5) | copy-start | bytes 1572868

commit v3 on v2

--- a/solution.py
+++ b/solution.py
@@ -17,10 +17,10 @@
 MESH = pl.DeviceIdType.MESH
 
 ORDER = (
-    ("G3a", "G2a", "T1a", "I1a", "T2a", "G2b", "T1b", "I1b", "T2b", "G3b", "I2b", "G0a", "I3a", "T3b", "I3b", "T3a", "I2a", "G0b", "G1a", "G1b"),
-    ("T0b", "T2a", "I0b", "T0a", "I0a", "T2b", "I2a", "I2b", "T3b", "G3a", "T3a", "G2a", "I3a", "G2b", "I3b", "G3b", "G1a", "G0a", "G0b", "G1b"),
-    ("T1b", "T1a", "T3b", "T3a", "I3a", "I1a", "T0b", "I3b", "G0a", "I1b", "I0a", "G1a", "I0b", "T0a", "G0b", "G1b", "G3a", "G2a", "G2b", "G3b"),
-    ("G0a", "G1a", "I2a", "I2b", "G0b", "T1a", "G1b", "I0a", "T1b", "T2b", "T0a", "G3a", "G2a", "I0b", "I1b", "I1a", "T0b", "T2a", "G2b", "G3b"),
+    ("G3a", "T1a", "G2a", "I1a", "T2a", "G3b", "T2b", "G2b", "T1b", "I3a", "G0a", "T3a", "I2a", "I1b", "T3b", "I3b", "G0b", "G1b", "I2b", "G1a"),
+    ("T0b", "T0a", "T2b", "I0a", "T2a", "I2a", "I2b", "I0b", "T3b", "G3a", "T3a", "I3a", "G2a", "I3b", "G3b", "G0a", "G1b", "G2b", "G0b", "G1a"),
+    ("T1a", "T3b", "T1b", "I1b", "T3a", "I3a", "T0b", "I3b", "I1a", "T0a", "G0a", "G1b", "I0b", "I0a", "G0b", "G3a", "G1a", "G2a", "G3b", "G2b"),
+    ("G0a", "G1b", "G1a", "T1a", "T2a", "G0b", "I1a", "I0b", "I0a", "T2b", "T0b", "T0a", "I2a", "G2a", "T1b", "I2b", "G3b", "G3a", "I1b", "G2b"),
 )
 CLASSES = {"T": TEXT, "I": NEAR, "G": FAR}
 PARTS = {"a": 0, "b": 1}
@@ -67,7 +67,14 @@
     return result
 
 
-def attend(queries, chunks, bias, tops, totals, sums, kind, chunk, first):
+def normalized(weighted, totals):
+    total = jnp.sum(totals, axis=1, keepdims=True)
+    positive = total > 0.0
+    inverse = jnp.where(positive, 1.0 / jnp.where(positive, total, 1.0), 0.0)
+    return (weighted * inverse).astype(jnp.bfloat16)
+
+
+def attend(queries, chunks, bias, tops, totals, sums, kind, chunk, first, results=None):
     for group in range(2):
         columns = slice(group * HEAD_DIM, (group + 1) * HEAD_DIM)
         keys = chunks[chunk, 0, :, :, :, columns].reshape(HEAD_DIM, HEAD_DIM)
@@ -91,19 +98,22 @@
             weighted = sums[kind, group] * factor + jnp.dot(
                 weights.astype(jnp.bfloat16), values, preferred_element_type=jnp.float32
             )
+        if results is not None:
+            scaled = normalized(weighted, total)
+            for head in range(8):
+                columns = slice((group * 8 + head) * HEAD_DIM, (group * 8 + head + 1) * HEAD_DIM)
+                results[1, :, columns] = scaled[head * 128 : (head + 1) * 128]
+            continue
         tops[kind, group] = new_top
         totals[kind, group] = total
         sums[kind, group] = weighted
 
 
-def finish(staged, totals, sums, kind):
+def finish(results, totals, sums, kind):
     for head in range(16):
         rows = slice((head % 8) * 128, (head % 8 + 1) * 128)
-        total = jnp.sum(totals[kind, head // 8, rows, :], axis=1, keepdims=True)
-        positive = total > 0.0
-        inverse = jnp.where(positive, 1.0 / jnp.where(positive, total, 1.0), 0.0)
-        result = sums[kind, head // 8, rows, :] * inverse
-        staged[kind, :, head * HEAD_DIM : (head + 1) * HEAD_DIM] = result.astype(jnp.bfloat16)
+        scaled = normalized(sums[kind, head // 8, rows, :], totals[kind, head // 8, rows, :])
+        results[kind, :, head * HEAD_DIM : (head + 1) * HEAD_DIM] = scaled
 
 
 def kernel(
@@ -114,13 +124,11 @@
     images,
     lengths_hbm,
     places_hbm,
-    self_out,
-    cross_out,
+    results,
     lengths,
     image_places,
     queries,
     chunks,
-    staged,
     bias,
     begins,
     tops,
@@ -129,6 +137,7 @@
     local_sems,
     send_sems,
     recv_sems,
+    far_ready,
 ):
     block = lax.axis_index("ctx")
     lane = lax.axis_index("tp")
@@ -141,6 +150,7 @@
     def at(step, to_lane):
         return (lax.rem(block + step + blocks, blocks), to_lane)
 
+    half = lane // 2
     first_row = block < ROW
     last_row = block >= blocks - ROW
 
@@ -167,19 +177,30 @@
     def _():
         greet(3, lane)
 
-    @pl.when((place >= 2) & last_row)
-    def _():
-        greet(0, far_lane)
-
-    @pl.when((place == 0) & ~first_row)
-    def _():
-        greet(-1, far_lane)
-        greet(-2, far_lane)
-
-    @pl.when(place == 3)
-    def _():
-        greet(-3, far_lane)
-        greet(-2, far_lane)
+    far_step = jnp.where(last_row, pick(place, FAR_STEP_LAST), pick(place, FAR_STEP))
+
+    @pl.when(half == 0)
+    def _():
+        greet(far_step, far_lane)
+
+    def for_far_sources(tell):
+        @pl.when((place >= 2) & last_row)
+        def _():
+            tell(0, far_lane)
+
+        @pl.when((place == 0) & ~first_row)
+        def _():
+            tell(-1, far_lane)
+            tell(-2, far_lane)
+
+        @pl.when(place == 3)
+        def _():
+            tell(-3, far_lane)
+            tell(-2, far_lane)
+
+    @pl.when(half == 0)
+    def _():
+        for_far_sources(greet)
 
     def columns(of_lane):
         return images.at[:, :, :, pl.ds(pl.multiple_of(of_lane * 256, 256), 256)]
@@ -190,8 +211,8 @@
         pltpu.make_async_copy(columns(far_lane), chunks.at[FAR + OWN, :, :, core], local_sems.at[2]),
         pltpu.make_async_copy(self_queries, queries.at[0], local_sems.at[3]),
         pltpu.make_async_copy(cross_queries, queries.at[1], local_sems.at[4]),
-        pltpu.make_async_copy(lengths_hbm, lengths, local_sems.at[7]),
-        pltpu.make_async_copy(places_hbm, image_places, local_sems.at[8]),
+        pltpu.make_async_copy(lengths_hbm, lengths, local_sems.at[5]),
+        pltpu.make_async_copy(places_hbm, image_places, local_sems.at[6]),
     ]
     for load in loads:
         load.start()
@@ -213,14 +234,14 @@
         seen = (positions >= begins[...]) & (positions <= token)
         bias[...] = jnp.where(seen, 0.0, HIDDEN)
 
-    def take(group, source, chunk, first):
+    def take(group, source, chunk, first, last_results=None):
         index = lax.broadcasted_iota(jnp.int32, (128, 128), 1)
         slot = jnp.maximum(source, 0) * 2
         left = jnp.where(source >= 0, image_places[slot], -1)
         right = jnp.where(source >= 0, image_places[slot + 1], -1)
         mask(jnp.where(group == TEXT, source * 128 + index, jnp.where(index < 64, left, right)))
         kind = jnp.where(group == TEXT, 0, 1)
-        attend(queries, chunks, bias, tops, totals, sums, kind, chunk, first)
+        attend(queries, chunks, bias, tops, totals, sums, kind, chunk, first, last_results)
 
     def send(source, target, sem, receive, device):
         return pltpu.make_async_remote_copy(
@@ -245,7 +266,17 @@
 
     expected = pick(place, (3, 6, 6, 4)) - jnp.where(last_row & (place >= 1), 1, 0)
     expected = expected - jnp.where(first_row & ((place == 1) | (place == 2)), 1, 0)
-    pl.semaphore_wait(barrier, expected)
+    far_sources = pick(place, (2, 0, 0, 2)) - jnp.where(first_row & (place == 0), 2, 0)
+    far_sources = far_sources + jnp.where(last_row & (place >= 2), 1, 0)
+    pl.semaphore_wait(barrier, expected + jnp.where(half == 0, -1, far_sources))
+
+    def invite(step, to_lane):
+        pl.semaphore_signal(far_ready, inc=1, device_id=at(step, to_lane), device_id_type=MESH)
+
+    @pl.when(half == 1)
+    def _():
+        for_far_sources(invite)
+
     own_near, own_far = NEAR + OWN, FAR + OWN
     swap_far = send(
         columns(other_far_lane), chunks.at[own_far, :, :, core], 0, recv_sems.at[own_far, 0], at(0, other_lane)
@@ -268,7 +299,6 @@
     start(sent)
     loads[2].wait()
     swap_far.wait_recv()
-    far_step = jnp.where(last_row, pick(place, FAR_STEP_LAST), pick(place, FAR_STEP))
     to_far = [
         send(
             chunks.at[own_far, part],
@@ -279,19 +309,30 @@
         )
         for part in range(2)
     ]
-    for copy in to_far:
-        copy.start()
+    @pl.when(half == 1)
+    def _():
+        for copy in to_far:
+            copy.start()
+
     loads[1].wait()
     swap_near.wait_recv()
     sent_near = list(sources_of_own(NEAR, 8))
     start(sent_near)
+
     sent += sent_near
     loads[3].wait()
     take(TEXT, block, TEXT + OWN, True)
+
+    @pl.when(half == 0)
+    def _():
+        pl.semaphore_wait(far_ready, 1)
+        for copy in to_far:
+            copy.start()
+
     loads[4].wait()
     take(NEAR, block, NEAR + OWN, True)
 
-    store_self = pltpu.make_async_copy(staged.at[0], self_out, local_sems.at[5])
+    taken, text_left, finished = 0, [ROW - 1] * ROW, False
     for number, (groups, sources, parts, steps, ready) in enumerate(plan()):
         group, source, part, step = (pick(place, table) for table in (groups, sources, parts, steps))
         chunk = group + source
@@ -300,10 +341,6 @@
             chunks.at[chunk, part], chunks.at[chunk, part], 12 + number, recv_sems.at[chunk, part], at(step, lane)
         )
         goes = (origin >= 0) & (step != 0) & ~((step == 3) & last_row)
-        if number == len(ORDER[0]) - 1:
-            finish(staged, totals, sums, 0)
-            store_self.start()
-
         @pl.when(origin >= 0)
         def _(forward=forward):
             forward.wait_recv()
@@ -316,14 +353,24 @@
         for whole_groups, whole_sources in ready:
             group, source = pick(place, whole_groups), pick(place, whole_sources)
             origin = block - place + source - jnp.where(source > place, ROW, 0)
+            taken += 1
+            last_results = results if taken == 10 else None
 
             @pl.when(origin >= 0)
-            def _(group=group, source=source, origin=origin):
-                take(group, origin, group + source, False)
-
-    finish(staged, totals, sums, 1)
-    store_cross = pltpu.make_async_copy(staged.at[1], cross_out, local_sems.at[6])
-    store_cross.start()
+            def _(group=group, source=source, origin=origin, last_results=last_results):
+                take(group, origin, group + source, False, last_results)
+
+            if last_results is not None:
+
+                @pl.when(origin < 0)
+                def _():
+                    finish(results, totals, sums, 1)
+
+            text_left = [left - (at_place == TEXT) for left, at_place in zip(text_left, whole_groups)]
+            if not finished and max(text_left) == 0:
+                finished = True
+                finish(results, totals, sums, 0)
+
     swap_near.wait_send()
     swap_far.wait_send()
     for copy in to_far:
@@ -334,33 +381,29 @@
         def _(copy=copy):
             copy.wait_send()
 
-    store_self.wait()
-    store_cross.wait()
-
 
 def per_device(self_queries, cross_queries, text_pairs, image_pairs, doc_lengths, image_places):
     anywhere = pl.BlockSpec(memory_space=pl.ANY)
-    result = jax.ShapeDtypeStruct(self_queries.shape, jnp.bfloat16)
     state = pltpu.VMEM((2, 2, 1024, HEAD_DIM), jnp.float32)
-    return pl.pallas_call(
+    results = pl.pallas_call(
         functools.partial(kernel, lax.axis_size("ctx")),
-        out_shape=(result, result),
+        out_shape=pltpu.VMEM((2, *self_queries.shape), jnp.bfloat16),
         in_specs=[anywhere] * 6,
-        out_specs=(anywhere, anywhere),
+        out_specs=pl.BlockSpec(memory_space=pltpu.VMEM),
         scratch_shapes=[
             pltpu.VMEM((1, 64), jnp.int32),
             pltpu.SMEM((256,), jnp.int32),
             pltpu.VMEM((2, 128, 2048), jnp.bfloat16),
             pltpu.VMEM((15, 2, 2, 2, 32, 256), jnp.bfloat16),
-            pltpu.VMEM((2, 128, 2048), jnp.bfloat16),
             pltpu.VMEM((128, 128), jnp.float32),
             pltpu.VMEM((128, 128), jnp.int32),
             state,
             state,
             state,
-            pltpu.SemaphoreType.DMA((9,)),
+            pltpu.SemaphoreType.DMA((7,)),
             pltpu.SemaphoreType.DMA((12 + len(ORDER[0]),)),
             pltpu.SemaphoreType.DMA((15, 2)),
+            pltpu.SemaphoreType.REGULAR,
         ],
         compiler_params=pltpu.CompilerParams(
             collective_id=0, has_side_effects=True, vmem_limit_bytes=60 << 20
@@ -373,6 +416,7 @@
         doc_lengths.reshape(1, 64),
         image_places,
     )
+    return results[0], results[1]
 
 
 def solution(mesh):

time: 43 us -> 40.2 us (0.935)
  the two profiles are of different devices: /device:TPU:230 before, /device:TPU:254 now
where the time goes in v3:
time: 40.2 us; the launch traced here: 40.1 us
  Pallas kernels  38.4 us (96%)
  local copies, waits for them, and re-layouts  1.08 us (3%)
  between operations  0.64 us (2%)
    pallas_call x1, Pallas kernels, per_device(): pl.pallas_call(functools.partial(kernel, lax.axis_size('ctx')), out_shape...  38.4 us
    squeeze x1, local copies, waits for them, and re-layouts, per_device(): return (results[0], results[1])  1.08 us

profile of v3, /device:TPU:254, one launch (start us, length us, event | category | flops | bytes accessed | tf_op | source)
XLA Modules:
  0.0 40.1 jit_solution(14531878896157414891)
XLA Ops:
  0.6 38.4 %shard_map.77 = bf16[2,128,2048]{2,1,0:T(8,128)(2,1)S(1)} custom-call(bf16[128,2048]{1,0:T(8,128)(2,1)} %self_queries.1, bf16[128,2048]{1,0:T(8,128)(2,1)} %cross_queries.1, bf16[2,2,2,32,256]{4,3,2,1,0:T(8,128)(2,1)} %bitcast.6, bf16[2,2,32,1024]{3,2,1,0:T(8,128)(2,1)} %images.1, s32[1,64]{1,0:T(1,128)} %bitcast.7, s32[256]{0:T(256)} %places_hbm.1), custom_call_target="tpu_custom_call" | custom-call | tf_op jit(solution)/shard_map/pallas_call | solution.py:388
  39.0 1.1 %slice_bitcast_fusion = (bf16[128,2048]{1,0:T(8,128)(2,1)}, bf16[128,2048]{1,0:T(8,128)(2,1)}) fusion(bf16[2,128,2048]{2,1,0:T(8,128)(2,1)S(1)} %shard_map.77), kind=kLoop, calls=%fused_computation | loop fusion | bytes 2097152 | tf_op jit(solution)/shard_map/squeeze | solution.py:419

commit v4 on v3

--- a/solution.py
+++ b/solution.py
@@ -17,10 +17,10 @@
 MESH = pl.DeviceIdType.MESH
 
 ORDER = (
-    ("G3a", "T1a", "G2a", "I1a", "T2a", "G3b", "T2b", "G2b", "T1b", "I3a", "G0a", "T3a", "I2a", "I1b", "T3b", "I3b", "G0b", "G1b", "I2b", "G1a"),
-    ("T0b", "T0a", "T2b", "I0a", "T2a", "I2a", "I2b", "I0b", "T3b", "G3a", "T3a", "I3a", "G2a", "I3b", "G3b", "G0a", "G1b", "G2b", "G0b", "G1a"),
-    ("T1a", "T3b", "T1b", "I1b", "T3a", "I3a", "T0b", "I3b", "I1a", "T0a", "G0a", "G1b", "I0b", "I0a", "G0b", "G3a", "G1a", "G2a", "G3b", "G2b"),
-    ("G0a", "G1b", "G1a", "T1a", "T2a", "G0b", "I1a", "I0b", "I0a", "T2b", "T0b", "T0a", "I2a", "G2a", "T1b", "I2b", "G3b", "G3a", "I1b", "G2b"),
+    ("G3a", "G2a", "T2b", "G2b", "T1b", "I1a", "T1a", "G3b", "I2b", "I3a", "I1b", "T3b", "I3b", "T2a", "T3a", "I2a", "G0a", "G1b", "G1a", "G0b"),
+    ("T0b", "T2a", "I0a", "I0b", "T2b", "I2a", "T0a", "T3b", "I2b", "G3a", "T3a", "I3a", "G2a", "I3b", "G2b", "G1b", "G3b", "G0a", "G1a", "G0b"),
+    ("T1a", "T3b", "I1a", "T3a", "I3a", "I3b", "T1b", "T0b", "I0a", "I1b", "G1b", "T0a", "G0a", "I0b", "G1a", "G3a", "G0b", "G2a", "G2b", "G3b"),
+    ("G0a", "G1b", "I2a", "I1a", "G1a", "G0b", "T0a", "I0a", "I2b", "I0b", "T0b", "T1a", "T1b", "G3a", "T2b", "I1b", "G2b", "T2a", "G2a", "G3b"),
 )
 CLASSES = {"T": TEXT, "I": NEAR, "G": FAR}
 PARTS = {"a": 0, "b": 1}

time: 40.2 us -> 39 us (0.970)
  the two profiles are of different devices: /device:TPU:254 before, /device:TPU:56 now
where the time goes in v4:
time: 39 us; the launch traced here: 38.9 us
  Pallas kernels  37.1 us (95%)
  local copies, waits for them, and re-layouts  1.08 us (3%)
  between operations  0.64 us (2%)
    pallas_call x1, Pallas kernels, per_device(): pl.pallas_call(functools.partial(kernel, lax.axis_size('ctx')), out_shape...  37.1 us
    squeeze x1, local copies, waits for them, and re-layouts, per_device(): return (results[0], results[1])  1.08 us

profile of v4, /device:TPU:56, one launch (start us, length us, event | category | flops | bytes accessed | tf_op | source)
XLA Modules:
  0.0 38.9 jit_solution(9129777416328944381)
XLA Ops:
  0.6 37.1 %shard_map.77 = bf16[2,128,2048]{2,1,0:T(8,128)(2,1)S(1)} custom-call(bf16[128,2048]{1,0:T(8,128)(2,1)} %self_queries.1, bf16[128,2048]{1,0:T(8,128)(2,1)} %cross_queries.1, bf16[2,2,2,32,256]{4,3,2,1,0:T(8,128)(2,1)} %bitcast.6, bf16[2,2,32,1024]{3,2,1,0:T(8,128)(2,1)} %images.1, s32[1,64]{1,0:T(1,128)} %bitcast.7, s32[256]{0:T(256)} %places_hbm.1), custom_call_target="tpu_custom_call" | custom-call | tf_op jit(solution)/shard_map/pallas_call | solution.py:388
  37.8 1.1 %slice_bitcast_fusion = (bf16[128,2048]{1,0:T(8,128)(2,1)}, bf16[128,2048]{1,0:T(8,128)(2,1)}) fusion(bf16[2,128,2048]{2,1,0:T(8,128)(2,1)S(1)} %shard_map.77), kind=kLoop, calls=%fused_computation | loop fusion | bytes 2097152 | tf_op jit(solution)/shard_map/squeeze | solution.py:419

commit v5 on v4

--- a/solution.py
+++ b/solution.py
@@ -19,8 +19,8 @@
 ORDER = (
     ("G3a", "G2a", "T2b", "G2b", "T1b", "I1a", "T1a", "G3b", "I2b", "I3a", "I1b", "T3b", "I3b", "T2a", "T3a", "I2a", "G0a", "G1b", "G1a", "G0b"),
     ("T0b", "T2a", "I0a", "I0b", "T2b", "I2a", "T0a", "T3b", "I2b", "G3a", "T3a", "I3a", "G2a", "I3b", "G2b", "G1b", "G3b", "G0a", "G1a", "G0b"),
-    ("T1a", "T3b", "I1a", "T3a", "I3a", "I3b", "T1b", "T0b", "I0a", "I1b", "G1b", "T0a", "G0a", "I0b", "G1a", "G3a", "G0b", "G2a", "G2b", "G3b"),
-    ("G0a", "G1b", "I2a", "I1a", "G1a", "G0b", "T0a", "I0a", "I2b", "I0b", "T0b", "T1a", "T1b", "G3a", "T2b", "I1b", "G2b", "T2a", "G2a", "G3b"),
+    ("T1a", "I1a", "I1b", "T3a", "T1b", "T3b", "I3a", "T0b", "T0a", "I3b", "G0a", "I0a", "I0b", "G1b", "G0b", "G3a", "G1a", "G2a", "G3b", "G2b"),
+    ("G0a", "G1b", "T1a", "G0b", "I2b", "I2a", "I1a", "G1a", "T0b", "T2b", "I1b", "T2a", "I0a", "T0a", "I0b", "G3a", "G2a", "T1b", "G3b", "G2b"),
 )
 CLASSES = {"T": TEXT, "I": NEAR, "G": FAR}
 PARTS = {"a": 0, "b": 1}

time: 39 us -> 38.8 us (level)
  the two profiles are of different devices: /device:TPU:56 before, /device:TPU:288 now
where the time goes in v5:
time: 38.8 us; the launch traced here: 38.7 us
  Pallas kernels  36.9 us (95%)
  local copies, waits for them, and re-layouts  1.08 us (3%)
  between operations  0.64 us (2%)
    pallas_call x1, Pallas kernels, per_device(): pl.pallas_call(functools.partial(kernel, lax.axis_size('ctx')), out_shape...  36.9 us
    squeeze x1, local copies, waits for them, and re-layouts, per_device(): return (results[0], results[1])  1.08 us

profile of v5, /device:TPU:288, one launch (start us, length us, event | category | flops | bytes accessed | tf_op | source)
XLA Modules:
  0.0 38.7 jit_solution(9220851952565260292)
XLA Ops:
  0.6 36.9 %shard_map.77 = bf16[2,128,2048]{2,1,0:T(8,128)(2,1)S(1)} custom-call(bf16[128,2048]{1,0:T(8,128)(2,1)} %self_queries.1, bf16[128,2048]{1,0:T(8,128)(2,1)} %cross_queries.1, bf16[2,2,2,32,256]{4,3,2,1,0:T(8,128)(2,1)} %bitcast.6, bf16[2,2,32,1024]{3,2,1,0:T(8,128)(2,1)} %images.1, s32[1,64]{1,0:T(1,128)} %bitcast.7, s32[256]{0:T(256)} %places_hbm.1), custom_call_target="tpu_custom_call" | custom-call | tf_op jit(solution)/shard_map/pallas_call | solution.py:388
  37.6 1.1 %slice_bitcast_fusion = (bf16[128,2048]{1,0:T(8,128)(2,1)}, bf16[128,2048]{1,0:T(8,128)(2,1)}) fusion(bf16[2,128,2048]{2,1,0:T(8,128)(2,1)S(1)} %shard_map.77), kind=kLoop, calls=%fused_computation | loop fusion | bytes 2097152 | tf_op jit(solution)/shard_map/squeeze | solution.py:419

commit v6 on v5

--- a/solution.py
+++ b/solution.py
@@ -254,8 +254,8 @@
         )
 
     def sources_of_own(group, sem):
-        for part in range(2):
-            for kind, (step, goes) in enumerate(((1, place <= 2), (3, (place >= 1) & ~last_row))):
+        for kind, (step, goes) in enumerate(((1, place <= 2), (3, (place >= 1) & ~last_row))):
+            for part in range(2):
                 yield goes, send(
                     chunks.at[group + OWN, part],
                     chunks.at[group + place, part],

time: 38.8 us -> 38.8 us (level)
  no operation moved by 1% of the time
where the time goes in v6:
time: 38.8 us; the launch traced here: 38.7 us
  Pallas kernels  36.9 us (95%)
  local copies, waits for them, and re-layouts  1.08 us (3%)
  between operations  0.64 us (2%)
    pallas_call x1, Pallas kernels, per_device(): pl.pallas_call(functools.partial(kernel, lax.axis_size('ctx')), out_shape...  36.9 us
    squeeze x1, local copies, waits for them, and re-layouts, per_device(): return (results[0], results[1])  1.08 us

profile of v6, /device:TPU:288, one launch (start us, length us, event | category | flops | bytes accessed | tf_op | source)
XLA Modules:
  0.0 38.7 jit_solution(9042013957248392221)
XLA Ops:
  0.6 36.9 %shard_map.77 = bf16[2,128,2048]{2,1,0:T(8,128)(2,1)S(1)} custom-call(bf16[128,2048]{1,0:T(8,128)(2,1)} %self_queries.1, bf16[128,2048]{1,0:T(8,128)(2,1)} %cross_queries.1, bf16[2,2,2,32,256]{4,3,2,1,0:T(8,128)(2,1)} %bitcast.6, bf16[2,2,32,1024]{3,2,1,0:T(8,128)(2,1)} %images.1, s32[1,64]{1,0:T(1,128)} %bitcast.7, s32[256]{0:T(256)} %places_hbm.1), custom_call_target="tpu_custom_call" | custom-call | tf_op jit(solution)/shard_map/pallas_call | solution.py:388
  37.6 1.1 %slice_bitcast_fusion = (bf16[128,2048]{1,0:T(8,128)(2,1)}, bf16[128,2048]{1,0:T(8,128)(2,1)}) fusion(bf16[2,128,2048]{2,1,0:T(8,128)(2,1)S(1)} %shard_map.77), kind=kLoop, calls=%fused_computation | loop fusion | bytes 2097152 | tf_op jit(solution)/shard_map/squeeze | solution.py:419
